TPU v7x, 32 devices: a whole 2x2x4 slice. The times are simulated.
32 devices in a mesh: groups: 2 (over y), req: 4 (over x, core), tensor: 4 (over z).
Axes of the slice: x: 2, y: 2, z: 4, core: 2. Of those that a mesh axis runs over, the one named last changes fastest.
Arguments:
- hidden: bfloat16 [384, 24576], P(('groups', 'req'), 'tensor'), parts along dimension 0, may hold values from -6 to 6
- join_weight: bfloat16 [24576, 8192], P('tensor', 'req'), may hold values from -0.0390625 to 0.0390625
- norm_gain: bfloat16 [8192], P(('req', 'tensor')), may hold values from 0.099609375 to 1.8984375
- qkv_weight: bfloat16 [8192, 9216], P(('req', 'tensor')), may hold values from -0.0625 to 0.0625
- owner_draft_cache: bfloat16 [48, 512, 2, 512], P(('groups', 'req'), 'tensor'), parts along dimension 0, may hold values from -250 to 250
- node_count: int32 [48], P('groups'), parts along dimension 0, may hold values from 1 to 8, as said below
- owner: int32 [48], P('groups'), parts along dimension 0, may hold values from 0 to 3, as said below
- cache_len: int32 [48], P('groups'), parts along dimension 0, may hold values from 1 to 512, as said below
Outputs:
- draft_attention: bfloat16 [48, 8, 8192], P(('groups', 'req'), None, 'tensor'), parts along dimension 0
There are 2 independent parts, one for each index of `groups`. A program takes and returns all parts, laid end to end along the dimension named above; an argument that names none is the same for every part. Nothing has to cross between parts.
Inputs may be any that keep to these rules, and one draw needn't show every extreme that they name: Every owner holds exactly 6 requests. `node_count`: some request has all 8 nodes live. `cache_len`: some slot uses all 512 positions.
All inputs are finite; a program needn't handle non-finite values.
Results may differ from a plain program's by a relative error of at most 0.01655.
The roundings to bfloat16 on the way count: a program that leaves them out, or rounds other values in their place, can miss the bound.
Values may be sent and summed in bfloat16 or wider, within the bound.
A program may use at most 256 MiB of HBM per device.

v0:
```python
import jax
import jax.numpy as jnp
from jax import lax
from jax.sharding import PartitionSpec as P

DF = 8192
QUERY_HEADS = 64
KEY_VALUE_HEADS = 4
HEAD_SIZE = 128
TREE_SLOTS = 8
CACHE_BLOCK = 128
norm_eps = 1e-05


def slots(owner, request_per_owner):
    count_all = owner.shape[0]
    same_owner = owner[:, None] == owner[None, :]
    earlier = jnp.arange(count_all)[None, :] < jnp.arange(count_all)[:, None]
    ranking = jnp.sum((same_owner & earlier).astype(jnp.int32), axis=1)
    return owner * request_per_owner + ranking


def body(
    hidden, join_weight, norm_gain, qkv_weight, owner_draft_cache, node_count, owner, cache_len
):
    tensor_count = lax.axis_size("tensor")
    req_here = lax.axis_index("req")
    tensor_here = lax.axis_index("tensor")
    request_per_owner = owner_draft_cache.shape[0]
    count_all = owner.shape[0]
    slot_of = slots(owner, request_per_owner)
    slot_table = slot_of[None, :] == jnp.arange(count_all, dtype=jnp.int32)[:, None]
    rows_all = count_all * TREE_SLOTS
    hidden_all = lax.all_gather(hidden, "req", axis=0, tiled=True)
    partial_sum = jnp.dot(hidden_all, join_weight, preferred_element_type=jnp.float32)
    joined = lax.psum_scatter(partial_sum, "tensor", scatter_dimension=1, tiled=True).astype(
        jnp.bfloat16
    )
    features = joined.shape[1]
    joined = jnp.dot(
        slot_table.astype(jnp.bfloat16),
        joined.reshape(count_all, TREE_SLOTS * features),
        preferred_element_type=jnp.float32,
    ).reshape(rows_all, features)
    scaled = (joined * norm_gain.astype(jnp.float32)).astype(jnp.bfloat16)
    partial_qkv = jnp.dot(scaled, qkv_weight, preferred_element_type=jnp.float32)
    row_squares = jnp.sum(joined * joined, axis=1)
    own_qkv = lax.psum_scatter(partial_qkv, "req", scatter_dimension=0, tiled=True)
    total_squares = lax.dynamic_slice_in_dim(
        lax.psum(row_squares, ("req", "tensor")),
        req_here * request_per_owner * TREE_SLOTS,
        request_per_owner * TREE_SLOTS,
    )
    total_qkv = lax.psum(own_qkv, "tensor")
    query_key_value = (total_qkv * lax.rsqrt(total_squares[:, None] / DF + norm_eps)).astype(
        jnp.bfloat16
    )
    query_group_width = QUERY_HEADS // KEY_VALUE_HEADS
    query_rows = query_key_value[:, : QUERY_HEADS * HEAD_SIZE].reshape(
        request_per_owner, TREE_SLOTS, KEY_VALUE_HEADS, query_group_width, HEAD_SIZE
    )
    fresh_key = query_key_value[
        :, QUERY_HEADS * HEAD_SIZE : (QUERY_HEADS + KEY_VALUE_HEADS) * HEAD_SIZE
    ].reshape(request_per_owner, TREE_SLOTS, KEY_VALUE_HEADS, HEAD_SIZE)
    fresh_value = query_key_value[:, (QUERY_HEADS + KEY_VALUE_HEADS) * HEAD_SIZE :].reshape(
        request_per_owner, TREE_SLOTS, KEY_VALUE_HEADS, HEAD_SIZE
    )
    cached_key_rows = owner_draft_cache[:, :, 0].reshape(
        request_per_owner, CACHE_BLOCK, KEY_VALUE_HEADS, HEAD_SIZE
    )
    cached_value_rows = owner_draft_cache[:, :, 1].reshape(
        request_per_owner, CACHE_BLOCK, KEY_VALUE_HEADS, HEAD_SIZE
    )
    lengths = lax.dynamic_slice_in_dim(cache_len, req_here * request_per_owner, request_per_owner)
    live_all = jnp.sum(jnp.where(slot_table, node_count[None, :], 0), axis=1)
    live_slot = lax.dynamic_slice_in_dim(live_all, req_here * request_per_owner, request_per_owner)
    scale_factor = HEAD_SIZE ** (-0.5)
    positions = tensor_here * CACHE_BLOCK + jnp.arange(CACHE_BLOCK)
    cache_mask = (positions[None, :] < lengths[:, None])[:, None, None, None, :]
    score_cache = (
        jnp.einsum(
            "snkgd,spkd->snkgp", query_rows, cached_key_rows, preferred_element_type=jnp.float32
        )
        * scale_factor
    )
    score_cache = jnp.where(cache_mask, score_cache, -1e30)
    first_block = tensor_here == 0
    new_mask = (jnp.arange(TREE_SLOTS)[None, :] <= jnp.arange(TREE_SLOTS)[:, None]) & first_block
    new_mask = new_mask[None, :, None, None, :]
    score_new = (
        jnp.einsum("snkgd,smkd->snkgm", query_rows, fresh_key, preferred_element_type=jnp.float32)
        * scale_factor
    )
    score_new = jnp.where(new_mask, score_new, -1e30)
    local_top = jnp.maximum(jnp.max(score_cache, axis=-1), jnp.max(score_new, axis=-1))
    top_score = lax.pmax(local_top, "tensor")
    weight_cache = jnp.where(cache_mask, jnp.exp(score_cache - top_score[..., None]), 0.0)
    weight_new = jnp.where(new_mask, jnp.exp(score_new - top_score[..., None]), 0.0)
    denominator = jnp.sum(weight_cache, axis=-1) + jnp.sum(weight_new, axis=-1)
    accum = jnp.einsum(
        "snkgp,spkd->snkgd",
        weight_cache.astype(jnp.bfloat16),
        cached_value_rows,
        preferred_element_type=jnp.float32,
    )
    accum = accum + jnp.einsum(
        "snkgm,smkd->snkgd",
        weight_new.astype(jnp.bfloat16),
        fresh_value,
        preferred_element_type=jnp.float32,
    )
    head_cols = QUERY_HEADS * HEAD_SIZE // tensor_count
    accum_all, denom_all = lax.psum((accum, denominator), "tensor")
    result_all = (accum_all / denom_all[..., None]).reshape(
        request_per_owner, TREE_SLOTS, QUERY_HEADS * HEAD_SIZE
    )
    result = lax.dynamic_slice_in_dim(result_all, tensor_here * head_cols, head_cols, 2)
    alive = (jnp.arange(TREE_SLOTS)[None, :] < live_slot[:, None])[:, :, None]
    return jnp.where(alive, result, 0.0).astype(jnp.bfloat16)


def solution(mesh):
    return jax.shard_map(
        body,
        mesh=mesh,
        in_specs=(
            P(("groups", "req"), "tensor"),
            P("tensor", "req"),
            P(("req", "tensor")),
            P(("req", "tensor"), None),
            P(("groups", "req"), "tensor", None, None),
            P("groups"),
            P("groups"),
            P("groups"),
        ),
        out_specs=P(("groups", "req"), None, "tensor"),
        check_vma=False,
    )
```

profile of v0, /device:TPU:0, one launch (start us, length us, event | category | flops | bytes accessed | tf_op | source)
XLA Modules:
  0.0 341.3 jit_solution(7624498871045635591)
XLA Ops:
  6.5 0.7 all-gather.2.cloned.1.call-update
  7.3 28.4 %all-gather.2.cloned.1.call-done = bf16[192,6144]{1,0:T(8,128)(2,1)} async-done(((bf16[48,6144]{1,0:T(8,128)(2,1)}), bf16[192,6144]{1,0:T(8,128)(2,1)}) %all-gather.2.cloned.1.call-update) | async-done | bytes 2359312 | tf_op jit(solution)/shard_map/all_gather | solution.py:34
  35.7 12.3 %fusion.29 = f32[192,2048]{1,0:T(8,128)} fusion(bf16[192,6144]{1,0:T(8,128)(2,1)} %all-gather.2.cloned.1.call-done, bf16[6144,2048]{1,0:T(8,128)(2,1)} %param.9), kind=kOutput, calls=%fused_computation.50 | convolution fusion | flops 4831838208 | bytes 29097984 | tf_op jit(solution)/shard_map/dot_general | solution.py:35
  48.1 0.6 copy-done.2
  48.7 0.2 convert_reduce_fusion
  48.9 34.6 %reduce-scatter.3.cloned.1.call-done = f32[192,512]{1,0:T(8,128)} async-done(((f32[192,2048]{1,0:T(8,128)}), f32[192,512]{1,0:T(8,128)}) %reduce-scatter.3.cloned.1.call-update) | async-done | bytes 393232 | tf_op jit(solution)/shard_map/reduce_scatter | solution.py:36
  83.5 1.0 convert_element_type.26
  84.6 0.2 fusion.21
  84.9 8.6 %fusion.19 = f32[192,9216]{1,0:T(8,128)} fusion(bf16[512,9216]{1,0:T(8,128)(2,1)} %param.11, f32[192,512]{1,0:T(8,128)S(1)} %reshape.91, f32[512]{0:T(512)S(1)} %convert_element_type.27), kind=kOutput, calls=%fused_computation.28 | convolution fusion | flops 1812135936 | bytes 16910336 | tf_op jit(solution)/shard_map/dot_general | solution.py:46
  93.6 62.7 %reduce-scatter.5.cloned.1.call-done = f32[48,9216]{1,0:T(8,128)} async-done(((f32[192,9216]{1,0:T(8,128)}), f32[48,9216]{1,0:T(8,128)}) %reduce-scatter.5.cloned.1.call-update) | async-done | bytes 1769488 | tf_op jit(solution)/shard_map/reduce_scatter | solution.py:48
  156.4 3.1 fusion.27
  159.5 4.7 %copy.33 = bf16[6,128,1,512]{1,3,0,2:T(8,128)(2,1)} copy(bf16[6,128,1,512]{3,2,1,0:T(2,128)(2,1)} %get-tuple-element.5) | data formatting | bytes 1572864
  164.1 2.6 copy.34
  166.9 0.1 multiply_reduce_fusion
  167.0 34.1 %psum.29 = f32[192]{0:T(256)S(1)} all-reduce(f32[192]{0:T(256)S(1)} %multiply_reduce_fusion), channel_id=1, replica_groups=mesh['groups'=2,'req'=4,'tensor'=4] {'req','tensor'}, use_global_device_ids=true, to_apply=%region_6.7 | all-reduce | flops 192 | bytes 1536 | tf_op jit(solution)/shard_map/psum | solution.py:50
  201.2 34.3 %all-reduce.3.cloned.1.call-done = f32[48,9216]{1,0:T(8,128)} async-done(((f32[48,9216]{1,0:T(8,128)}), f32[48,9216]{1,0:T(8,128)}) %all-reduce.3.cloned.1.call-update) | async-done | bytes 1769488 | tf_op jit(solution)/shard_map/psum | solution.py:54
  235.5 1.6 multiply_convert_fusion
  237.2 2.0 fusion.28
  239.1 0.6 bitcast_reduce_fusion
  239.8 18.5 %pmax.7 = f32[6,8,4,16]{3,1,2,0:T(8,128)S(1)} all-reduce(f32[6,8,4,16]{3,1,2,0:T(8,128)S(1)} %max.5), channel_id=1, replica_groups=mesh['groups'=2,'req'=4,'tensor'=4] {'tensor'}, use_global_device_ids=true, to_apply=%region_9.10 | all-reduce | flops 3072 | bytes 24576 | tf_op jit(solution)/shard_map/pmax | solution.py:96
  258.3 1.7 fusion.6
  260.0 1.8 bitcast_add_fusion
  261.8 0.6 copy-done.5
  262.5 0.1 select_reduce_fusion
  262.7 0.4 fusion.13
  263.1 0.9 fusion.4
  264.0 21.0 %psum.31 = f32[6,8,4,16]{3,1,2,0:T(8,128)S(1)} all-reduce(f32[6,8,4,16]{3,1,2,0:T(8,128)S(1)} %add.56), channel_id=1, replica_groups=mesh['groups'=2,'req'=4,'tensor'=4] {'tensor'}, use_global_device_ids=true, to_apply=%region_13.14 | all-reduce | flops 3072 | bytes 24576 | tf_op jit(solution)/shard_map/psum | solution.py:113
  285.0 46.5 %all-reduce.5.cloned.1.call-done = f32[6,8,4,16,128]{4,3,1,2,0:T(8,128)} async-done(((f32[6,8,4,16,128]{4,3,1,2,0:T(8,128)}), f32[6,8,4,16,128]{4,3,1,2,0:T(8,128)}) %all-reduce.5.cloned.1.call-update) | async-done | bytes 1572880 | tf_op jit(solution)/shard_map/psum | solution.py:113
  331.5 1.9 broadcast_divide_fusion
  333.4 0.2 copy.24
  333.6 0.3 reshape.95
  334.0 0.8 select_convert_fusion
  (33 shorter events, 0.9 us)
Async XLA Ops:
  6.5 29.2 %all-gather.2.cloned.1.call-start = ((), (), s32[]{:S(2)}) async-start(), calls=%async_computation.2 | async-start | bytes 2949120 | tf_op jit(solution)/shard_map/all_gather | solution.py:34
  7.3 76.3 %reduce-scatter.3.cloned.1.call-start = ((), (), s32[]{:S(2)}) async-start(), calls=%async_computation.3 | async-start | bytes 1966080 | tf_op jit(solution)/shard_map/reduce_scatter | solution.py:36
  48.0 0.7 copy-start.2
  48.0 0.7 copy-start.3
  48.1 108.2 %reduce-scatter.5.cloned.1.call-start = ((), (), s32[]{:S(2)}) async-start(), calls=%async_computation.4 | async-start | bytes 8847360 | tf_op jit(solution)/shard_map/reduce_scatter | solution.py:48
  93.6 62.8 %copy-start = (bf16[6,128,2,512]{3,2,1,0:T(2,128)(2,1)S(1)}, bf16[6,128,2,512]{3,2,1,0:T(2,128)(2,1)}, u32[]{:S(2)}) copy-start(bf16[6,128,2,512]{3,2,1,0:T(2,128)(2,1)} %param.12) | copy-start | bytes 4718596
  93.6 141.9 %all-reduce.3.cloned.1.call-start = ((), (), s32[]{:S(2)}) async-start(), calls=%async_computation.5 | async-start | bytes 3538944 | tf_op jit(solution)/shard_map/psum | solution.py:54
  156.3 175.2 %all-reduce.5.cloned.1.call-start = ((), (), s32[]{:S(2)}) async-start(), calls=%async_computation.6 | async-start | bytes 3145728 | tf_op jit(solution)/shard_map/psum | solution.py:113
  164.1 2.6 copy-start.4
  237.1 2.0 copy-start.1
  261.8 0.7 copy-start.5
Sparse Core Ops, SparseCore 0:
  8.9 26.7 all-gather.1
  48.2 35.2 reduce-scatter.2
  93.7 62.5 reduce-scatter.4
  158.7 76.7 all-reduce.2
  261.9 69.5 all-reduce.4
where the time goes:
time: 342 us; the launch traced here: 341 us
  waiting for transfers between devices  207 us (61%)
  blocking collectives  73.6 us (22%)
  matrix products  27.2 us (8%)
  between operations  13.3 us (4%)
  local copies, waits for them, and re-layouts  12.5 us (4%)
  other arithmetic  7.31 us (2%)
    reduce_scatter x1, waiting for transfers between devices, body(): lax.psum_scatter(partial_qkv, 'req', scatter_dimension=0, tiled=True)  62.7 us
    psum x1, waiting for transfers between devices, body(): accum_all, denom_all = lax.psum((accum, denominator), 'tensor')  46.5 us
    reduce_scatter x1, waiting for transfers between devices, body(): lax.psum_scatter(partial_sum, 'tensor', scatter_dimension=1, tiled=True)  34.6 us
    psum x1, waiting for transfers between devices, body(): total_qkv = lax.psum(own_qkv, 'tensor')  34.3 us
    psum x1, blocking collectives, body(): lax.psum(row_squares, ('req', 'tensor'))  34.1 us
    all_gather x1, waiting for transfers between devices, body(): hidden_all = lax.all_gather(hidden, 'req', axis=0, tiled=True)  28.4 us
    psum x1, blocking collectives, body(): accum_all, denom_all = lax.psum((accum, denominator), 'tensor')  21 us
    pmax x1, blocking collectives, body(): top_score = lax.pmax(local_top, 'tensor')  18.5 us
  transfers between devices with their start and end apart: 5, of which 5 were waited for; matrix products, arithmetic and copies ran while one was open for 4% of the time, Pallas kernels for 0%

commit v1 on v0

--- a/solution.py
+++ b/solution.py
@@ -10,6 +10,29 @@
 TREE_SLOTS = 8
 CACHE_BLOCK = 128
 norm_eps = 1e-05
+
+
+def laid_out(pieces, dim):
+    pieces = jnp.moveaxis(pieces, 0, dim)
+    shape = pieces.shape
+    return pieces.reshape(*shape[:dim], shape[dim] * shape[dim + 1], *shape[dim + 2 :])
+
+
+def doubled(shard, axis):
+    size, position = (lax.axis_size(axis), lax.axis_index(axis))
+    blocks, distance = (shard[None], 1)
+    while distance < size:
+        received = lax.ppermute(blocks, axis, [(i, i ^ distance) for i in range(size)])
+        low = position & distance == 0
+        blocks = jnp.concatenate(
+            [jnp.where(low, blocks, received), jnp.where(low, received, blocks)]
+        )
+        distance *= 2
+    return blocks
+
+
+def doubled_up(shard, axis, dim):
+    return laid_out(doubled(shard, axis), dim)
 
 
 def slots(owner, request_per_owner):
@@ -31,7 +54,7 @@
     slot_of = slots(owner, request_per_owner)
     slot_table = slot_of[None, :] == jnp.arange(count_all, dtype=jnp.int32)[:, None]
     rows_all = count_all * TREE_SLOTS
-    hidden_all = lax.all_gather(hidden, "req", axis=0, tiled=True)
+    hidden_all = doubled_up(hidden, "req", 0)
     partial_sum = jnp.dot(hidden_all, join_weight, preferred_element_type=jnp.float32)
     joined = lax.psum_scatter(partial_sum, "tensor", scatter_dimension=1, tiled=True).astype(
         jnp.bfloat16

time: 342 us -> 347 us (1.015)
    all_gather x1 -> x0, waiting for transfers between devices: 28.4 us -> none  [body(): hidden_all = lax.all_gather(hidden, 'req', axis=0, tiled=True)]
    ppermute x0 -> x2, waiting for transfers between devices: none -> 28.1 us  [doubled(): lax.ppermute(blocks, axis, [(i, i ^ distance) for i in range(size)])]
  transfers between devices with their start and end apart: 5 -> 6, of which waited for: 5 -> 6; matrix products, arithmetic and copies ran while one was open for 4% -> 4% of each run, Pallas kernels for 0% -> 0%
where the time goes in v1:
time: 347 us
  waiting for transfers between devices  208 us (60%)
  blocking collectives  73.5 us (21%)
  matrix products  26.9 us (8%)
  between operations  13.3 us (4%)
  local copies, waits for them, and re-layouts  12.5 us (4%)
  other arithmetic  8.92 us (3%)
  starting transfers between devices  3.5 us (1%)
    reduce_scatter x1, waiting for transfers between devices, body(): lax.psum_scatter(partial_qkv, 'req', scatter_dimension=0, tiled=True)  62.7 us
    psum x1, waiting for transfers between devices, body(): accum_all, denom_all = lax.psum((accum, denominator), 'tensor')  46.5 us
    reduce_scatter x1, waiting for transfers between devices, body(): lax.psum_scatter(partial_sum, 'tensor', scatter_dimension=1, tiled=True)  36.1 us
    psum x1, waiting for transfers between devices, body(): total_qkv = lax.psum(own_qkv, 'tensor')  34.5 us
    psum x1, blocking collectives, body(): lax.psum(row_squares, ('req', 'tensor'))  34.1 us
    ppermute x2, waiting for transfers between devices, doubled(): lax.ppermute(blocks, axis, [(i, i ^ distance) for i in range(size)])  28.1 us
    psum x1, blocking collectives, body(): accum_all, denom_all = lax.psum((accum, denominator), 'tensor')  21 us
    pmax x1, blocking collectives, body(): top_score = lax.pmax(local_top, 'tensor')  18.5 us
  transfers between devices with their start and end apart: 6, of which 6 were waited for; matrix products, arithmetic and copies ran while one was open for 4% of the time, Pallas kernels for 0%

profile of v1, /device:TPU:0, one launch (start us, length us, event | category | flops | bytes accessed | tf_op | source)
XLA Modules:
  0.0 346.6 jit_solution(164357499398489799)
XLA Ops:
  6.5 0.5 collective-permute-start
  7.0 1.8 collective-permute-done
  8.8 1.1 broadcast_select_fusion.3
  10.1 2.9 collective-permute-start.1
  13.0 26.3 %collective-permute-done.1 = bf16[2,48,6144]{2,1,0:T(8,128)(2,1)S(1)} collective-permute-done((bf16[2,48,6144]{2,1,0:T(8,128)(2,1)S(1)}, bf16[2,48,6144]{2,1,0:T(8,128)(2,1)S(1)}, u32[]{:S(2)}, u32[]{:S(2)}) %collective-permute-start.1) | collective-permute-done | bytes 1179680 | tf_op jit(solution)/shard_map/ppermute | solution.py:25
  39.5 0.2 pad_maximum_fusion
  39.7 12.0 %fusion.29 = f32[192,2048]{1,0:T(8,128)} fusion(bf16[192,6144]{1,0:T(8,128)(2,1)S(1)} %bitcast.63, bf16[6144,2048]{1,0:T(8,128)(2,1)} %param.9), kind=kOutput, calls=%fused_computation.56 | convolution fusion | flops 4831838208 | bytes 29097984 | tf_op jit(solution)/shard_map/dot_general | solution.py:58
  51.7 0.6 copy-done.2
  52.5 36.1 %reduce-scatter.3.cloned.1.call-done = f32[192,512]{1,0:T(8,128)} async-done(((f32[192,2048]{1,0:T(8,128)}), f32[192,512]{1,0:T(8,128)}) %reduce-scatter.3.cloned.1.call-update) | async-done | bytes 393232 | tf_op jit(solution)/shard_map/reduce_scatter | solution.py:59
  88.6 1.0 convert_element_type.26
  90.0 8.6 %fusion.19 = f32[192,9216]{1,0:T(8,128)} fusion(bf16[512,9216]{1,0:T(8,128)(2,1)} %param.11, f32[192,512]{1,0:T(8,128)S(1)} %reshape.95, f32[512]{0:T(512)S(1)} %convert_element_type.27), kind=kOutput, calls=%fused_computation.34 | convolution fusion | flops 1812135936 | bytes 16910336 | tf_op jit(solution)/shard_map/dot_general | solution.py:69
  98.7 62.7 %reduce-scatter.5.cloned.1.call-done = f32[48,9216]{1,0:T(8,128)} async-done(((f32[192,9216]{1,0:T(8,128)}), f32[48,9216]{1,0:T(8,128)}) %reduce-scatter.5.cloned.1.call-update) | async-done | bytes 1769488 | tf_op jit(solution)/shard_map/reduce_scatter | solution.py:71
  161.5 3.1 fusion.27
  164.6 4.7 %copy.33 = bf16[6,128,1,512]{1,3,0,2:T(8,128)(2,1)} copy(bf16[6,128,1,512]{3,2,1,0:T(2,128)(2,1)} %get-tuple-element.7) | data formatting | bytes 1572864
  169.2 2.6 copy.34
  172.1 34.1 %psum.29 = f32[192]{0:T(256)S(1)} all-reduce(f32[192]{0:T(256)S(1)} %multiply_reduce_fusion), channel_id=1, replica_groups=mesh['groups'=2,'req'=4,'tensor'=4] {'req','tensor'}, use_global_device_ids=true, to_apply=%region_6.7 | all-reduce | flops 192 | bytes 1536 | tf_op jit(solution)/shard_map/psum | solution.py:73
  206.3 34.5 %all-reduce.3.cloned.1.call-done = f32[48,9216]{1,0:T(8,128)} async-done(((f32[48,9216]{1,0:T(8,128)}), f32[48,9216]{1,0:T(8,128)}) %all-reduce.3.cloned.1.call-update) | async-done | bytes 1769488 | tf_op jit(solution)/shard_map/psum | solution.py:77
  240.7 1.6 multiply_convert_fusion
  242.4 2.0 fusion.28
  244.4 0.6 bitcast_reduce_fusion
  245.1 18.5 %pmax.7 = f32[6,8,4,16]{3,1,2,0:T(8,128)S(1)} all-reduce(f32[6,8,4,16]{3,1,2,0:T(8,128)S(1)} %max.5), channel_id=1, replica_groups=mesh['groups'=2,'req'=4,'tensor'=4] {'tensor'}, use_global_device_ids=true, to_apply=%region_9.10 | all-reduce | flops 3072 | bytes 24576 | tf_op jit(solution)/shard_map/pmax | solution.py:119
  263.6 1.7 fusion.6
  265.3 1.8 bitcast_add_fusion
  267.1 0.6 copy-done.5
  268.0 0.4 fusion.13
  268.4 0.9 fusion.4
  269.3 21.0 %psum.31 = f32[6,8,4,16]{3,1,2,0:T(8,128)S(1)} all-reduce(f32[6,8,4,16]{3,1,2,0:T(8,128)S(1)} %add.56), channel_id=1, replica_groups=mesh['groups'=2,'req'=4,'tensor'=4] {'tensor'}, use_global_device_ids=true, to_apply=%region_13.14 | all-reduce | flops 3072 | bytes 24576 | tf_op jit(solution)/shard_map/psum | solution.py:136
  290.3 46.5 %all-reduce.5.cloned.1.call-done = f32[6,8,4,16,128]{4,3,1,2,0:T(8,128)} async-done(((f32[6,8,4,16,128]{4,3,1,2,0:T(8,128)}), f32[6,8,4,16,128]{4,3,1,2,0:T(8,128)}) %all-reduce.5.cloned.1.call-update) | async-done | bytes 1572880 | tf_op jit(solution)/shard_map/psum | solution.py:136
  336.8 1.9 broadcast_divide_fusion
  338.7 0.2 copy.24
  338.9 0.3 reshape.99
  339.3 0.8 select_convert_fusion
  (38 shorter events, 1.7 us)
Async XLA Ops:
  6.5 82.1 %reduce-scatter.3.cloned.1.call-start = ((), (), s32[]{:S(2)}) async-start(), calls=%async_computation.2 | async-start | bytes 1966080 | tf_op jit(solution)/shard_map/reduce_scatter | solution.py:59
  6.5 2.3 collective-permute-start
  10.1 29.2 %collective-permute-start.1 = (bf16[2,48,6144]{2,1,0:T(8,128)(2,1)S(1)}, bf16[2,48,6144]{2,1,0:T(8,128)(2,1)S(1)}, u32[]{:S(2)}, u32[]{:S(2)}) collective-permute-start(bf16[2,48,6144]{2,1,0:T(8,128)(2,1)S(1)} %pad_maximum_fusion.1), channel_id=1, source_target_pairs={{0,8},{4,12},{8,0},{12,4},{1,9},{5,13},{9,1},{13,5},{2,10},{6,14},... | collective-permute-start | bytes 3538952 | tf_op jit(solution)/shard_map/ppermute | solution.py:25
  51.7 0.7 copy-start.2
  51.7 0.7 copy-start.3
  51.7 109.7 %reduce-scatter.5.cloned.1.call-start = ((), (), s32[]{:S(2)}) async-start(), calls=%async_computation.3 | async-start | bytes 8847360 | tf_op jit(solution)/shard_map/reduce_scatter | solution.py:71
  98.7 62.8 %copy-start = (bf16[6,128,2,512]{3,2,1,0:T(2,128)(2,1)S(1)}, bf16[6,128,2,512]{3,2,1,0:T(2,128)(2,1)}, u32[]{:S(2)}) copy-start(bf16[6,128,2,512]{3,2,1,0:T(2,128)(2,1)} %param.12) | copy-start | bytes 4718596
  98.7 142.0 %all-reduce.3.cloned.1.call-start = ((), (), s32[]{:S(2)}) async-start(), calls=%async_computation.4 | async-start | bytes 3538944 | tf_op jit(solution)/shard_map/psum | solution.py:77
  161.4 175.4 %all-reduce.5.cloned.1.call-start = ((), (), s32[]{:S(2)}) async-start(), calls=%async_computation.5 | async-start | bytes 3145728 | tf_op jit(solution)/shard_map/psum | solution.py:136
  169.2 2.6 copy-start.4
  242.4 2.0 copy-start.1
  267.1 0.7 copy-start.5
Sparse Core Ops, SparseCore 0:
  51.8 36.7 reduce-scatter.2
  98.8 62.5 reduce-scatter.4
  163.9 76.7 all-reduce.2
  267.2 69.5 all-reduce.4
